TPU v7x, 32 devices: a whole 2x2x4 slice. The times are simulated.
32 devices in a mesh: space: 8 (over z, x), blk: 4 (over y, core).
Axes of the slice: x: 2, y: 2, z: 4, core: 2. Of those that a mesh axis runs over, the one named last changes fastest.
Arguments:
- snapshots: float32 [32, 256, 5, 2048], P('blk', 'space'), may hold values from -72 to 72
- weights: float32 [5, 2048], P(None, 'space'), may hold values from 0.05 to 31, as said below
- frequencies: int32 [16], replicated, may hold values from 0 to 127, as said below
- offsets: int32 [32], P('blk'), may hold values from 0 to 4095
- eigenvectors: float32 [16, 2, 32, 4], replicated, may hold values from -6 to 6
Outputs:
- modes: float32 [16, 2, 4, 5, 2048], P('blk', None, None, None, 'space')
- energies: float32 [16, 4], P('blk')
Inputs may be any that keep to these rules, and one draw needn't show every extreme that they name: `weights`: positive. `frequencies`: distinct indices.
All inputs are finite; a program needn't handle non-finite values.
Results may differ from a plain program's by a relative error of at most 0.000073.
Values sent between devices are 32-bit elements; how exact they have to be, the bound alone decides.
A program may use at most 384 MiB of HBM per device.

v0:
```python
import math

import jax
import jax.numpy as jnp
from jax import lax
from jax.sharding import PartitionSpec as P

HIGH = lax.Precision.HIGHEST


def projection(snap_shape, frequencies, offsets, eigenvectors, count, dtype=jnp.float32):
    items, times = snap_shape[0], snap_shape[1]
    num_freq = frequencies.shape[0]
    all_times = jnp.arange(count, dtype=jnp.int32)
    phases = 2.0 * math.pi / count * all_times.astype(jnp.float32)
    window = 0.5 - 0.5 * jnp.cos(phases)
    norm = jnp.sqrt(jnp.sum(window * window))
    own = lax.axis_index("space") * times + jnp.arange(times, dtype=jnp.int32)
    own_window = (0.5 - 0.5 * jnp.cos(2.0 * math.pi / count * own.astype(jnp.float32))) / norm
    shifted = (own[None, :] + offsets[:, None]) % count
    turns = frequencies[:, None, None] * shifted[None] % count
    angles = 2.0 * math.pi / count * turns.astype(jnp.float32)
    cosine = own_window * jnp.cos(angles)
    sine = -own_window * jnp.sin(angles)
    vec = lax.dynamic_slice_in_dim(eigenvectors, lax.axis_index("blk") * items, items, 2)
    vec = vec.transpose(0, 1, 3, 2)[..., None]
    vec_real, vec_imag = vec[:, 0], vec[:, 1]
    cosine, sine = cosine[:, None], sine[:, None]
    real = vec_real * cosine - vec_imag * sine
    imag = vec_real * sine + vec_imag * cosine
    return jnp.stack([real, imag], axis=1)


def local(snapshots, weights, frequencies, offsets, eigenvectors):
    num_blocks = eigenvectors.shape[2]
    count = snapshots.shape[1] * lax.axis_size("space")
    matrix = projection(snapshots.shape, frequencies, offsets, eigenvectors, count)
    partial = jnp.einsum("fpmbt,btvc->fpmvc", matrix, snapshots, precision=HIGH)
    part = lax.psum_scatter(partial, "blk", scatter_dimension=0, tiled=True)
    unscaled = lax.psum_scatter(part, "space", scatter_dimension=4, tiled=True)
    local_energy = jnp.sum(unscaled * unscaled * weights, axis=(1, 3, 4))
    energy, total = lax.psum((local_energy, jnp.sum(weights)), "space")
    energies = energy / (num_blocks * total)
    divisor = jnp.sqrt(num_blocks * energies + 1e-06)
    modes = unscaled / divisor[:, None, :, None, None]
    return (modes, energies)


def solution(mesh):
    in_specs = (P("blk", "space", None, None), P(None, "space"), P(), P("blk"), P())
    out_specs = (P("blk", None, None, None, "space"), P("blk", None))
    return jax.shard_map(local, mesh=mesh, in_specs=in_specs, out_specs=out_specs, check_vma=False)
```

profile of v0, /device:TPU:0, one launch (start us, length us, event | category | flops | bytes accessed | tf_op | source)
XLA Modules:
  0.0 337.5 jit_solution(15332680963598051285)
XLA Ops:
  7.2 0.0 copy-start
  7.2 0.0 all-reduce.4.cloned.1.call-start
  7.2 0.6 multiply_reduce_fusion.1
  7.9 0.1 copy-done
  8.0 0.1 dynamic-slice_bitcast_fusion
  8.1 0.1 copy.12
  8.2 0.1 copy.13
  9.0 0.1 fusion.14
  9.1 0.7 add_select_fusion.2
  9.8 1.0 cosine_multiply_fusion
  10.8 0.2 multiply_subtract_fusion
  11.0 18.5 %fusion.2 = f32[16,2,4,5,2048]{4,0,3,2,1:T(8,128)} fusion(f32[8,32,5,2048]{3,1,2,0:T(8,128)} %param.5, f32[16,1,4,8,32]{4,0,3,2,1:T(8,128)S(1)} %get-tuple-element.13, f32[16,1,4,8,32]{4,0,3,2,1:T(8,128)S(1)} %get-tuple-element.12), kind=kOutput, calls=%fused_computation.2 | convolution fusion | flops 4026564608 | bytes 15859712 | tf_op jit(solution)/shard_map/fpmbt,btvc->fpmvc/dot_general | solution.py:38
  29.5 0.0 copy-start.2
  29.5 0.0 all-reduce.4.cloned.1.call-update
  29.6 0.0 reduce-scatter.5.cloned.1.call-start
  29.6 0.6 copy-done.2
  30.2 0.6 dynamic-slice
  31.4 103.5 %all-reduce.4.cloned.1.call-done = f32[16,2,4,5,2048]{4,0,3,2,1:T(8,128)} async-done(((f32[16,2,4,5,2048]{4,0,3,2,1:T(8,128)}), f32[16,2,4,5,2048]{4,0,3,2,1:T(8,128)}) %all-reduce.4.cloned.1.call-update) | async-done | bytes 5242896
  135.0 2.1 constant_dynamic-slice_fusion
  137.0 50.8 %copy.24 = f32[4,2,4,5,2048]{0,3,2,1,4:T(8,128)} copy(f32[4,2,4,5,2048]{4,0,3,2,1:T(4,128)S(1)} %constant_dynamic-slice_fusion) | data formatting | bytes 2621440
  187.8 40.7 %reshape.104 = f32[2048,160]{1,0:T(8,128)} reshape(f32[2048,2,4,5,4]{4,3,2,1,0:T(8,128)} %bitcast.11) | data formatting | bytes 2621440
  228.6 0.0 reduce-scatter.5.cloned.1.call-update
  228.6 0.0 copy-done.1
  228.6 0.6 reduce_sum.29
  229.2 67.3 %reduce-scatter.5.cloned.1.call-done = f32[256,160]{1,0:T(8,128)} async-done(((f32[2048,160]{1,0:T(8,128)}), f32[256,160]{1,0:T(8,128)}) %reduce-scatter.5.cloned.1.call-update) | async-done | bytes 163856
  296.5 6.8 %reshape.105 = f32[256,2,4,5,4]{4,3,2,1,0:T(8,128)} reshape(f32[256,160]{1,0:T(8,128)} %reduce-scatter.5.cloned.1.call-done) | data formatting | bytes 327680
  303.3 5.3 %copy.25 = f32[4,2,4,5,256]{4,0,3,2,1:T(4,128)S(1)} copy(f32[4,2,4,5,256]{0,3,2,1,4:T(8,128)} %bitcast.29) | data formatting | bytes 327680
  308.6 0.1 multiply_reduce_fusion
  308.8 19.7 %all-reduce.1 = (f32[4,4]{0,1:T(4,128)S(1)}, f32[]{:T(128)}) all-reduce(f32[4,4]{0,1:T(4,128)S(1)} %multiply_reduce_fusion, f32[]{:T(128)} %reduce_sum.29), channel_id=1, replica_groups=mesh['space'=8,'blk'=4] {'space'}, use_global_device_ids=true, to_apply=%region_4.5 | all-reduce | flops 17 | bytes 136 | tf_op jit(solution)/shard_map/psum | solution.py:42
  329.2 0.1 broadcast_divide_fusion
  329.3 0.7 copy.15
  330.0 0.7 copy.16
  (4 shorter events, 0.0 us)
Async XLA Ops:
  7.2 0.8 copy-start
  7.2 127.8 %all-reduce.4.cloned.1.call-start = ((), (), s32[]{:S(2)}) async-start(), calls=%async_computation.2 | async-start | bytes 10485760
  29.5 0.7 copy-start.2
  29.6 266.9 %reduce-scatter.5.cloned.1.call-start = ((), (), s32[]{:S(2)}) async-start(), calls=%async_computation.1 | async-start | bytes 2359296
  187.8 40.8 %copy-start.1 = (f32[5,256]{1,0:T(8,128)S(1)}, f32[5,256]{1,0:T(8,128)}, u32[]{:S(2)}) copy-start(f32[5,256]{1,0:T(8,128)} %param.6) | copy-start | bytes 15364
Sparse Core Ops, SparseCore 0:
  29.7 105.2 all-reduce.3
  228.7 67.7 reduce-scatter.4
where the time goes:
time: 338 us; the launch traced here: 337 us
  waiting for transfers between devices  171 us (51%)
  local copies, waits for them, and re-layouts  109 us (32%)
  blocking collectives  19.7 us (6%)
  matrix products  18.5 us (5%)
  between operations  16.1 us (5%)
  other arithmetic  3.5 us (1%)
    unnamed x4, waiting for transfers between devices  171 us
    unnamed x14, local copies, waits for them, and re-layouts  108 us
    psum x1, blocking collectives, local(): energy, total = lax.psum((local_energy, jnp.sum(weights)), 'space')  19.7 us
    dot_general x1, matrix products, local(): partial = jnp.einsum('fpmbt,btvc->fpmvc', matrix, snapshots, precision=HIGH)  18.5 us
  transfers between devices with their start and end apart: 2, of which 2 were waited for; matrix products, arithmetic and copies ran while one was open for 0% of the time, Pallas kernels for 0%

commit v1 on v0

--- a/solution.py
+++ b/solution.py
@@ -1,8 +1,11 @@
+import functools
 import math
 
 import jax
 import jax.numpy as jnp
 from jax import lax
+from jax.experimental import pallas as pl
+from jax.experimental.pallas import tpu as pltpu
 from jax.sharding import PartitionSpec as P
 
 HIGH = lax.Precision.HIGHEST
@@ -31,7 +34,7 @@
     return jnp.stack([real, imag], axis=1)
 
 
-def local(snapshots, weights, frequencies, offsets, eigenvectors):
+def local_plain(snapshots, weights, frequencies, offsets, eigenvectors):
     num_blocks = eigenvectors.shape[2]
     count = snapshots.shape[1] * lax.axis_size("space")
     matrix = projection(snapshots.shape, frequencies, offsets, eigenvectors, count)
@@ -46,7 +49,261 @@
     return (modes, energies)
 
 
+MESH = pl.DeviceIdType.MESH
+LANES = 128
+
+
+def reduce_kernel(
+    depth, x_ref, a_ref, w_ref, out_ref, e_ref,
+    xbuf, acat, keep, send0, r0, r1, r2, s2, r3, acc, esend, erecv,
+    x_sem, s0_sem, t0_sem, s1_sem, t1_sem, s2_sem, t2_sem, s3_sem, t3_sem, se_sem, te_sem,
+):
+    num_vars = w_ref.shape[0]
+    width = out_ref.shape[2]
+    rows = a_ref.shape[2]
+    half = rows // 2
+    total_rows = 4 * rows
+    inner = a_ref.shape[3]
+    space, blk = lax.axis_index("space"), lax.axis_index("blk")
+    z, x = space // 2, space % 2
+    y, c = blk // 2, blk % 2
+    size = 2 * depth
+    across_core = (space, y * 2 + (1 - c))
+    across_x = (z * 2 + (1 - x), blk)
+    across_y = (space, (1 - y) * 2 + c)
+
+    loads = []
+    for v in range(num_vars):
+        load = pltpu.make_async_copy(x_ref.at[:, v], xbuf.at[v], x_sem.at[v])
+        load.start()
+        loads.append(load)
+
+    barrier = pltpu.get_barrier_semaphore()
+    pl.semaphore_signal(barrier, inc=1, device_id=across_core, device_id_type=MESH)
+    pl.semaphore_signal(barrier, inc=1, device_id=across_y, device_id_type=MESH)
+    for d in range(1, size):
+        pl.semaphore_signal(
+            barrier, inc=1, device_id=(lax.rem(space + d, size), blk), device_id_type=MESH
+        )
+
+    for cr in range(2):
+        for yr in range(2):
+            part = a_ref[(y + yr) % 2, (c + cr) % 2]
+            high = part.astype(jnp.bfloat16)
+            low = (part - high.astype(jnp.float32)).astype(jnp.bfloat16)
+            first = (cr * 2 + yr) * rows
+            acat[first : first + rows, :] = high
+            acat[total_rows + first : total_rows + first + rows, :] = low
+
+    def project(v):
+        def column(k, carry):
+            for xa in range(2):
+                xr = (x + xa) % 2
+                cols = pl.ds(pl.multiple_of(k * (2 * width) + xa * width, width), width)
+                block = xbuf[v, :, :, cols].reshape(inner, width)
+                high = block.astype(jnp.bfloat16)
+                low = (block - high.astype(jnp.float32)).astype(jnp.bfloat16)
+                both = jnp.dot(acat[...], high, preferred_element_type=jnp.float32)
+                rest = jnp.dot(acat[:total_rows, :], low, preferred_element_type=jnp.float32)
+                res = both[:total_rows] + (both[total_rows:] + rest)
+                for cr, buf in ((0, keep), (1, send0)):
+                    for yr in range(2):
+                        first = (cr * 2 + yr) * rows
+                        buf[v, 0, xr, yr, k] = res[first : first + half]
+                        buf[v, 1, yr, xr, k] = res[first + half : first + rows]
+            return carry
+
+        lax.fori_loop(0, depth, column, 0)
+
+    def remote(src, dst, sem_out, sem_in, target):
+        return pltpu.make_async_remote_copy(
+            src_ref=src, dst_ref=dst, send_sem=sem_out, recv_sem=sem_in,
+            device_id=target, device_id_type=MESH,
+        )
+
+    hop0 = [
+        remote(send0.at[v], r0.at[v], s0_sem.at[v], t0_sem.at[v], across_core)
+        for v in range(num_vars)
+    ]
+    hop1 = [
+        [
+            remote(keep.at[v, h, 1], r1.at[v, h], s1_sem.at[v, h], t1_sem.at[v, h], to)
+            for h, to in ((0, across_x), (1, across_y))
+        ]
+        for v in range(num_vars)
+    ]
+    hop2 = [
+        [
+            remote(r1.at[v, h, 1], r2.at[v, h], s2_sem.at[v, h], t2_sem.at[v, h], to)
+            for h, to in ((0, across_y), (1, across_x))
+        ]
+        for v in range(num_vars)
+    ]
+    hop3 = []
+    for v in range(num_vars):
+        group = []
+        for d in range(1, depth):
+            k = lax.rem(z + d, depth)
+            group.append(
+                remote(
+                    s2.at[v, k], r3.at[v, d - 1], s3_sem.at[v, d - 1], t3_sem.at[v, d - 1],
+                    (k * 2 + x, blk),
+                )
+            )
+        hop3.append(group)
+
+    def stage0(v):
+        loads[v].wait()
+        project(v)
+        if v == 0:
+            pl.semaphore_wait(barrier, size + 1)
+        hop0[v].start()
+
+    def stage1(v):
+        hop0[v].wait_recv()
+        for h in range(2):
+            keep[v, h, 1] = keep[v, h, 1] + r0[v, h, 1]
+            hop1[v][h].start()
+
+    def stage2(v):
+        for h in range(2):
+            hop1[v][h].wait_recv()
+            r1[v, h, 1] = r1[v, h, 1] + (keep[v, h, 0, 1] + r0[v, h, 0, 1])
+            hop2[v][h].start()
+
+    def stage3(v):
+        for h in range(2):
+            hop2[v][h].wait_recv()
+            s2[v, :, h] = (keep[v, h, 0, 0] + r0[v, h, 0, 0]) + (r1[v, h, 0] + r2[v, h])
+        for copy in hop3[v]:
+            copy.start()
+
+    def stage4(v):
+        for copy in hop3[v]:
+            copy.wait_recv()
+        result = s2[v, z]
+        for d in range(1, depth):
+            result = result + r3[v, d - 1]
+        result = result.reshape(rows, width)
+        out_ref[v] = result
+        term = result * result * w_ref[v : v + 1, :]
+        if v == 0:
+            acc[...] = term
+        else:
+            acc[...] = acc[...] + term
+
+    stages = (stage0, stage1, stage2, stage3, stage4)
+    for step in range(num_vars + len(stages) - 1):
+        for lag, stage in enumerate(stages):
+            if 0 <= step - lag < num_vars:
+                stage(step - lag)
+
+    def fold(value):
+        folded = value[:, :LANES]
+        for k in range(1, width // LANES):
+            folded = folded + value[:, k * LANES : (k + 1) * LANES]
+        return folded
+
+    esend[:rows, :] = fold(acc[...])
+    weight_sum = fold(jnp.sum(w_ref[...], axis=0, keepdims=True))
+    esend[rows:, :] = jnp.broadcast_to(weight_sum, (8, LANES))
+    share = []
+    for d in range(1, size):
+        copy = remote(
+            esend, erecv.at[d - 1], se_sem.at[d - 1], te_sem.at[d - 1],
+            (lax.rem(space + d, size), blk),
+        )
+        copy.start()
+        share.append(copy)
+    total = esend[...]
+    for d in range(1, size):
+        share[d - 1].wait_recv()
+        total = total + erecv[d - 1]
+    e_ref[...] = total
+    for v in range(num_vars):
+        hop0[v].wait_send()
+        for copy in hop1[v] + hop2[v] + hop3[v]:
+            copy.wait_send()
+    for copy in share:
+        copy.wait_send()
+
+
+def reduce_modes(snapshots, matrix, weights):
+    items, num_vars, times, cells = snapshots.shape
+    width = weights.shape[1]
+    depth = cells // width // 2
+    rows = matrix.shape[2]
+    inner = matrix.shape[3]
+    half = rows // 2
+    size = 2 * depth
+    f32 = jnp.float32
+    dma = pltpu.SemaphoreType.DMA
+    vmem = pl.BlockSpec(memory_space=pltpu.VMEM)
+    return pl.pallas_call(
+        functools.partial(reduce_kernel, depth),
+        out_shape=(
+            jax.ShapeDtypeStruct((num_vars, rows, width), f32),
+            jax.ShapeDtypeStruct((rows + 8, LANES), f32),
+        ),
+        in_specs=[pl.BlockSpec(memory_space=pl.ANY), vmem, vmem],
+        out_specs=(vmem, vmem),
+        scratch_shapes=[
+            pltpu.VMEM((num_vars, items, times, cells), f32),
+            pltpu.VMEM((8 * rows, inner), jnp.bfloat16),
+            pltpu.VMEM((num_vars, 2, 2, 2, depth, half, width), f32),
+            pltpu.VMEM((num_vars, 2, 2, 2, depth, half, width), f32),
+            pltpu.VMEM((num_vars, 2, 2, 2, depth, half, width), f32),
+            pltpu.VMEM((num_vars, 2, 2, depth, half, width), f32),
+            pltpu.VMEM((num_vars, 2, depth, half, width), f32),
+            pltpu.VMEM((num_vars, depth, 2, half, width), f32),
+            pltpu.VMEM((num_vars, depth - 1, 2, half, width), f32),
+            pltpu.VMEM((rows, width), f32),
+            pltpu.VMEM((rows + 8, LANES), f32),
+            pltpu.VMEM((size - 1, rows + 8, LANES), f32),
+            dma((num_vars,)),
+            dma((num_vars,)),
+            dma((num_vars,)),
+            dma((num_vars, 2)),
+            dma((num_vars, 2)),
+            dma((num_vars, 2)),
+            dma((num_vars, 2)),
+            dma((num_vars, depth - 1)),
+            dma((num_vars, depth - 1)),
+            dma((size - 1,)),
+            dma((size - 1,)),
+        ],
+        compiler_params=pltpu.CompilerParams(
+            collective_id=0, has_side_effects=True, vmem_limit_bytes=56 * 2**20
+        ),
+    )(snapshots, matrix, weights)
+
+
+def local_kernel(snapshots, weights, frequencies, offsets, eigenvectors):
+    num_blocks = eigenvectors.shape[2]
+    num_freq = frequencies.shape[0]
+    modes_kept = eigenvectors.shape[3]
+    owned = num_freq // 4
+    num_vars, width = weights.shape
+    count = snapshots.shape[1] * lax.axis_size("space")
+    matrix = projection(snapshots.shape, frequencies, offsets, eigenvectors, count)
+    matrix = matrix.reshape(2, 2, owned * 2 * modes_kept, -1)
+    raw, sums = reduce_modes(snapshots.transpose(0, 2, 1, 3), matrix, weights)
+    rows = matrix.shape[2]
+    lane_sum = jnp.sum(sums, axis=1)
+    energy = jnp.sum(lane_sum[:rows].reshape(owned, 2, modes_kept), axis=1)
+    energies = energy / (num_blocks * lane_sum[rows])
+    divisor = jnp.sqrt(num_blocks * energies + 1e-06)
+    unscaled = raw.reshape(num_vars, owned, 2, modes_kept, width).transpose(1, 2, 3, 0, 4)
+    modes = unscaled / divisor[:, None, :, None, None]
+    return (modes, energies)
+
+
+def fits(mesh):
+    return mesh.shape["blk"] == 4 and mesh.shape["space"] == 8
+
+
 def solution(mesh):
+    local = local_kernel if fits(mesh) else local_plain
     in_specs = (P("blk", "space", None, None), P(None, "space"), P(), P("blk"), P())
     out_specs = (P("blk", None, None, None, "space"), P("blk", None))
     return jax.shard_map(local, mesh=mesh, in_specs=in_specs, out_specs=out_specs, check_vma=False)

time: 338 us -> 54 us (0.16)
  waiting for transfers between devices: 171 us -> 0 us
  local copies, waits for them, and re-layouts: 109 us -> 2.59 us
  Pallas kernels: 0 us -> 44.2 us
  blocking collectives: 19.7 us -> 0 us
  matrix products: 18.5 us -> 0 us
  between operations: 16.1 us -> 2.05 us
    unnamed x4 -> x0, waiting for transfers between devices: 171 us -> none
    unnamed x14 -> x2, local copies, waits for them, and re-layouts: 108 us -> 0.01 us
    pallas_call x0 -> x1, Pallas kernels: none -> 44.2 us  [reduce_modes(): pl.pallas_call(functools.partial(reduce_kernel, depth), out_shape=(jax.Sh...]
    psum x1 -> x0, blocking collectives: 19.7 us -> none  [local(): energy, total = lax.psum((local_energy, jnp.sum(weights)), 'space')]
    dot_general x1 -> x0, matrix products: 18.5 us -> none  [local(): partial = jnp.einsum('fpmbt,btvc->fpmvc', matrix, snapshots, precision=HIGH)]
  transfers between devices with their start and end apart: 2 -> 0, of which waited for: 2 -> 0; matrix products, arithmetic and copies ran while one was open for 0% -> 0% of each run, Pallas kernels for 0% -> 0%
where the time goes in v1:
time: 54 us; the launch traced here: 53.7 us
  Pallas kernels  44.2 us (82%)
  other arithmetic  4.89 us (9%)
  local copies, waits for them, and re-layouts  2.59 us (5%)
  between operations  2.05 us (4%)
    pallas_call x1, Pallas kernels, reduce_modes(): pl.pallas_call(functools.partial(reduce_kernel, depth), out_shape=(jax.Sh...  44.2 us

profile of v1, /device:TPU:0, one launch (start us, length us, event | category | flops | bytes accessed | tf_op | source)
XLA Modules:
  0.0 53.7 jit_solution(13034714581356140679)
XLA Ops:
  0.6 0.0 copy-start
  0.6 0.6 %multiply_reduce_fusion = f32[]{:T(128)} fusion(), kind=kLoop, calls=%fused_computation.26 | loop fusion | flops 1535 | bytes 4 | tf_op jit(solution)/shard_map/reduce_sum | solution.py:20
  2.1 0.7 %add_select_fusion.2 = s32[8,32]{1,0:T(8,128)S(1)} fusion(s32[8]{0:T(128)} %param.8, s32[32]{0:T(128)S(1)} %iota_add_fusion), kind=kLoop, calls=%fused_computation.21 | loop fusion | flops 3072 | bytes 1184 | tf_op jit(solution)/shard_map/jit(remainder)/select_n | solution.py:23
  2.8 0.0 copy-done
  2.8 0.1 dynamic-slice_bitcast_fusion
  2.9 1.0 %cosine_multiply_fusion = (f32[16,8,32]{2,1,0:T(8,128)S(1)}, f32[16,8,32]{2,1,0:T(8,128)S(1)}) fusion(s32[8,32]{1,0:T(8,128)S(1)} %add_select_fusion.2, s32[16]{0:T(128)} %param.7, f32[32]{0:T(128)S(1)} %get-tuple-element.9, f32[32]{0:T(128)S(1)} %get-tuple-element.8), kind=kLoop, calls=%fused_computation.14 | loop fusion | flops 65536 | bytes 34112 | tf_op jit(solution)/shard_map/mul | solution.py:26
  3.9 0.2 multiply_subtract_fusion
  4.2 0.8 %reshape.122.a_ref = f32[2,2,32,256]{3,2,1,0:T(8,128)} reshape(f32[16,2,4,8,32]{4,3,2,1,0:T(8,128)S(1)} %pad_maximum_fusion) | data formatting | bytes 262144 | tf_op jit(solution)/shard_map/reshape | solution.py:289
  5.0 44.2 %shard_map.68 = (f32[5,32,256]{2,1,0:T(8,128)}, f32[40,128]{1,0:T(8,128)}) custom-call(f32[8,5,32,2048]{3,2,1,0:T(8,128)} %bitcast.15, f32[2,2,32,256]{3,2,1,0:T(8,128)} %reshape.122.a_ref, f32[5,256]{1,0:T(8,128)} %w_ref.1), custom_call_target="tpu_custom_call" | custom-call | tf_op jit(solution)/shard_map/pallas_call | solution.py:242
  49.2 1.0 %reshape.123 = f32[5,4,2,4,256]{4,3,2,1,0:T(4,128)S(1)} reshape(f32[5,32,256]{2,1,0:T(8,128)} %get-tuple-element.4) | data formatting | bytes 327680 | tf_op jit(solution)/shard_map/reshape | solution.py:296
  50.2 0.8 %reduce_sum.28 = f32[40]{0:T(128)S(1)} reduce(f32[40,128]{1,0:T(8,128)} %get-tuple-element.5, f32[]{:T(128)} %constant.47.clone.1), dimensions={1}, to_apply=%region_1.2 | reduce | flops 5080 | bytes 20644 | tf_op jit(solution)/shard_map/reduce_sum | solution.py:292
  51.0 0.6 %slice.23 = f32[1]{0:T(128)} slice(f32[40]{0:T(128)S(1)} %reduce_sum.28), slice={[32:33]} | slice | bytes 8 | tf_op jit(solution)/shard_map/slice | solution.py:294
  52.3 0.1 reshape.124
  52.4 0.6 %add_sqrt_fusion = (f32[4,4]{1,0:T(4,128)S(1)}, f32[4,4]{1,0:T(4,128)}) fusion(f32[4,4]{1,0:T(4,128)S(1)} %reduce_sum.29, f32[]{:T(128)} %bitcast.6), kind=kLoop, calls=%fused_computation.24 | loop fusion | flops 48 | bytes 196 | tf_op jit(solution)/shard_map/sqrt | solution.py:295
  53.0 0.8 %fusion = f32[4,2,4,5,256]{4,2,3,1,0:T(4,128)} fusion(f32[5,4,2,4,256]{4,3,2,1,0:T(4,128)S(1)} %reshape.123, f32[4,4]{1,0:T(4,128)S(1)} %get-tuple-element.6), kind=kLoop, calls=%fused_computation.4 | loop fusion | flops 40960 | bytes 327744 | tf_op jit(solution)/shard_map/div | solution.py:297
  (5 shorter events, 0.1 us)
Async XLA Ops:
  0.6 2.2 %copy-start = (f32[16,2,32,4]{2,3,1,0:T(4,128)S(1)}, f32[16,2,32,4]{2,3,1,0:T(4,128)}, u32[]{:S(2)}) copy-start(f32[16,2,32,4]{2,3,1,0:T(4,128)} %param.9) | copy-start | bytes 49156

commit v2 on v1

--- a/solution.py
+++ b/solution.py
@@ -53,17 +53,50 @@
 LANES = 128
 
 
+def projection_rows(freq_ref, off_ref, vec, times, parts, space, blk):
+    num_freq, items = freq_ref.shape[0], off_ref.shape[0]
+    modes_kept, num_blocks = vec.shape[2], vec.shape[3]
+    count, inner = times * parts, items * times
+    lane = lax.broadcasted_iota(jnp.int32, (1, inner), 1)
+    block = lane // times
+    own = lane % times + space * times
+    shift = jnp.zeros_like(lane)
+    for b in range(items):
+        shift = jnp.where(block == b, off_ref[b], shift)
+    row = lax.broadcasted_iota(jnp.int32, (num_freq, inner), 0)
+    index = jnp.zeros_like(row)
+    for f in range(num_freq):
+        index = jnp.where(row == f, freq_ref[f], index)
+    turns = (index * ((own + shift) & (count - 1))) & (count - 1)
+    angles = 2.0 * math.pi / count * turns.astype(jnp.float32)
+    norm = math.sqrt(sum((0.5 - 0.5 * math.cos(2.0 * math.pi * t / count)) ** 2 for t in range(count)))
+    phases = 2.0 * math.pi / count * own.astype(jnp.float32)
+    window = (0.5 - 0.5 * jnp.cos(phases)) * (1.0 / norm)
+    full = (num_freq, 2 * modes_kept, inner)
+    cosine = jnp.broadcast_to((window * jnp.cos(angles))[:, None, :], full)
+    sine = jnp.broadcast_to((-window * jnp.sin(angles))[:, None, :], full)
+    pick = lax.broadcasted_iota(jnp.int32, (num_blocks, inner), 0) == block + blk * items
+    pick = jnp.where(pick, 1.0, 0.0)
+    turned = jnp.concatenate([-vec[:, 1:2], vec[:, 0:1]], axis=1)
+    flat = (num_freq * 2 * modes_kept, num_blocks)
+    straight = jnp.dot(vec.reshape(flat), pick, precision=HIGH, preferred_element_type=jnp.float32)
+    turned = jnp.dot(turned.reshape(flat), pick, precision=HIGH, preferred_element_type=jnp.float32)
+    flat = (num_freq * 2 * modes_kept, inner)
+    return straight * cosine.reshape(flat) + turned * sine.reshape(flat)
+
+
 def reduce_kernel(
-    depth, x_ref, a_ref, w_ref, out_ref, e_ref,
-    xbuf, acat, keep, send0, r0, r1, r2, s2, r3, acc, esend, erecv,
-    x_sem, s0_sem, t0_sem, s1_sem, t1_sem, s2_sem, t2_sem, s3_sem, t3_sem, se_sem, te_sem,
+    depth, num_blocks, x_ref, w_hbm, vec_hbm, freq_hbm, off_hbm, out_ref, energy_ref,
+    xbuf, w_ref, vec_ref, freq_ref, off_ref, raw, acat, keep, send0, r0, r1, r2, s2, r3, acc, esend, erecv,
+    in_sem, x_sem, s0_sem, t0_sem, s1_sem, t1_sem, s2_sem, t2_sem, s3_sem, t3_sem, se_sem, te_sem,
 ):
     num_vars = w_ref.shape[0]
-    width = out_ref.shape[2]
-    rows = a_ref.shape[2]
+    width = w_ref.shape[1]
+    num_freq, modes_kept = vec_ref.shape[0], vec_ref.shape[2]
+    total_rows = num_freq * 2 * modes_kept
+    rows = total_rows // 4
     half = rows // 2
-    total_rows = 4 * rows
-    inner = a_ref.shape[3]
+    inner = xbuf.shape[1] * xbuf.shape[2]
     space, blk = lax.axis_index("space"), lax.axis_index("blk")
     z, x = space // 2, space % 2
     y, c = blk // 2, blk % 2
@@ -72,6 +105,13 @@
     across_x = (z * 2 + (1 - x), blk)
     across_y = (space, (1 - y) * 2 + c)
 
+    small = []
+    for k, (src, dst) in enumerate(
+        ((freq_hbm, freq_ref), (off_hbm, off_ref), (vec_hbm, vec_ref), (w_hbm, w_ref))
+    ):
+        copy = pltpu.make_async_copy(src, dst, in_sem.at[k])
+        copy.start()
+        small.append(copy)
     loads = []
     for v in range(num_vars):
         load = pltpu.make_async_copy(x_ref.at[:, v], xbuf.at[v], x_sem.at[v])
@@ -86,14 +126,18 @@
             barrier, inc=1, device_id=(lax.rem(space + d, size), blk), device_id_type=MESH
         )
 
-    for cr in range(2):
-        for yr in range(2):
-            part = a_ref[(y + yr) % 2, (c + cr) % 2]
-            high = part.astype(jnp.bfloat16)
-            low = (part - high.astype(jnp.float32)).astype(jnp.bfloat16)
-            first = (cr * 2 + yr) * rows
-            acat[first : first + rows, :] = high
-            acat[total_rows + first : total_rows + first + rows, :] = low
+    for copy in small:
+        copy.wait()
+    matrix = projection_rows(
+        freq_ref, off_ref, vec_ref[...], xbuf.shape[2], 2 * depth, space, blk
+    )
+    high = matrix.astype(jnp.bfloat16)
+    low = (matrix - high.astype(jnp.float32)).astype(jnp.bfloat16)
+    for ya in range(2):
+        for ca in range(2):
+            first = (ya * 2 + ca) * rows
+            acat[0, (ca + c) % 2, (ya + y) % 2] = high[first : first + rows]
+            acat[1, (ca + c) % 2, (ya + y) % 2] = low[first : first + rows]
 
     def project(v):
         def column(k, carry):
@@ -103,8 +147,8 @@
                 block = xbuf[v, :, :, cols].reshape(inner, width)
                 high = block.astype(jnp.bfloat16)
                 low = (block - high.astype(jnp.float32)).astype(jnp.bfloat16)
-                both = jnp.dot(acat[...], high, preferred_element_type=jnp.float32)
-                rest = jnp.dot(acat[:total_rows, :], low, preferred_element_type=jnp.float32)
+                both = jnp.dot(acat[...].reshape(2 * total_rows, inner), high, preferred_element_type=jnp.float32)
+                rest = jnp.dot(acat[0].reshape(total_rows, inner), low, preferred_element_type=jnp.float32)
                 res = both[:total_rows] + (both[total_rows:] + rest)
                 for cr, buf in ((0, keep), (1, send0)):
                     for yr in range(2):
@@ -185,7 +229,7 @@
         for d in range(1, depth):
             result = result + r3[v, d - 1]
         result = result.reshape(rows, width)
-        out_ref[v] = result
+        raw[v] = result
         term = result * result * w_ref[v : v + 1, :]
         if v == 0:
             acc[...] = term
@@ -219,7 +263,20 @@
     for d in range(1, size):
         share[d - 1].wait_recv()
         total = total + erecv[d - 1]
-    e_ref[...] = total
+    owned = rows // (2 * modes_kept)
+    pair = total[:rows].reshape(owned, 2 * modes_kept, LANES)
+    pair = pair + jnp.concatenate([pair[:, modes_kept:], pair[:, :modes_kept]], axis=1)
+    weight_total = jnp.sum(total[rows : rows + 1], axis=1, keepdims=True)
+    energy = jnp.sum(pair, axis=2, keepdims=True) / (num_blocks * weight_total)[None]
+    inverse = 1.0 / jnp.sqrt(num_blocks * energy + 1e-06)
+    for v in range(num_vars):
+        scaled = raw[v].reshape(owned, 2 * modes_kept, width) * inverse
+        out_ref[:, 0, v] = scaled[:, :modes_kept]
+        out_ref[:, 1, v] = scaled[:, modes_kept:]
+    square = (modes_kept, modes_kept)
+    same = lax.broadcasted_iota(jnp.int32, square, 0) == lax.broadcasted_iota(jnp.int32, square, 1)
+    spread = jnp.broadcast_to(energy[:, :modes_kept], (owned, modes_kept, modes_kept))
+    energy_ref[...] = jnp.sum(jnp.where(same[None], spread, 0.0), axis=1)
     for v in range(num_vars):
         hop0[v].wait_send()
         for copy in hop1[v] + hop2[v] + hop3[v]:
@@ -228,28 +285,36 @@
         copy.wait_send()
 
 
-def reduce_modes(snapshots, matrix, weights):
+def reduce_modes(snapshots, weights, vectors, frequencies, offsets):
     items, num_vars, times, cells = snapshots.shape
+    num_freq, _, modes_kept, num_blocks = vectors.shape
     width = weights.shape[1]
     depth = cells // width // 2
-    rows = matrix.shape[2]
-    inner = matrix.shape[3]
+    owned = num_freq // 4
+    rows = owned * 2 * modes_kept
+    inner = items * times
     half = rows // 2
     size = 2 * depth
     f32 = jnp.float32
     dma = pltpu.SemaphoreType.DMA
+    anywhere = pl.BlockSpec(memory_space=pl.ANY)
     vmem = pl.BlockSpec(memory_space=pltpu.VMEM)
     return pl.pallas_call(
-        functools.partial(reduce_kernel, depth),
+        functools.partial(reduce_kernel, depth, num_blocks),
         out_shape=(
-            jax.ShapeDtypeStruct((num_vars, rows, width), f32),
-            jax.ShapeDtypeStruct((rows + 8, LANES), f32),
+            jax.ShapeDtypeStruct((owned, 2, num_vars, modes_kept, width), f32),
+            jax.ShapeDtypeStruct((owned, modes_kept), f32),
         ),
-        in_specs=[pl.BlockSpec(memory_space=pl.ANY), vmem, vmem],
+        in_specs=[anywhere] * 5,
         out_specs=(vmem, vmem),
         scratch_shapes=[
             pltpu.VMEM((num_vars, items, times, cells), f32),
-            pltpu.VMEM((8 * rows, inner), jnp.bfloat16),
+            pltpu.VMEM((num_vars, width), f32),
+            pltpu.VMEM(vectors.shape, f32),
+            pltpu.SMEM(frequencies.shape, jnp.int32),
+            pltpu.SMEM(offsets.shape, jnp.int32),
+            pltpu.VMEM((num_vars, rows, width), f32),
+            pltpu.VMEM((2, 2, 2, rows, inner), jnp.bfloat16),
             pltpu.VMEM((num_vars, 2, 2, 2, depth, half, width), f32),
             pltpu.VMEM((num_vars, 2, 2, 2, depth, half, width), f32),
             pltpu.VMEM((num_vars, 2, 2, 2, depth, half, width), f32),
@@ -260,6 +325,7 @@
             pltpu.VMEM((rows, width), f32),
             pltpu.VMEM((rows + 8, LANES), f32),
             pltpu.VMEM((size - 1, rows + 8, LANES), f32),
+            dma((4,)),
             dma((num_vars,)),
             dma((num_vars,)),
             dma((num_vars,)),
@@ -275,27 +341,15 @@
         compiler_params=pltpu.CompilerParams(
             collective_id=0, has_side_effects=True, vmem_limit_bytes=56 * 2**20
         ),
-    )(snapshots, matrix, weights)
+    )(snapshots, weights, vectors, frequencies, offsets)
 
 
 def local_kernel(snapshots, weights, frequencies, offsets, eigenvectors):
-    num_blocks = eigenvectors.shape[2]
-    num_freq = frequencies.shape[0]
-    modes_kept = eigenvectors.shape[3]
-    owned = num_freq // 4
-    num_vars, width = weights.shape
-    count = snapshots.shape[1] * lax.axis_size("space")
-    matrix = projection(snapshots.shape, frequencies, offsets, eigenvectors, count)
-    matrix = matrix.reshape(2, 2, owned * 2 * modes_kept, -1)
-    raw, sums = reduce_modes(snapshots.transpose(0, 2, 1, 3), matrix, weights)
-    rows = matrix.shape[2]
-    lane_sum = jnp.sum(sums, axis=1)
-    energy = jnp.sum(lane_sum[:rows].reshape(owned, 2, modes_kept), axis=1)
-    energies = energy / (num_blocks * lane_sum[rows])
-    divisor = jnp.sqrt(num_blocks * energies + 1e-06)
-    unscaled = raw.reshape(num_vars, owned, 2, modes_kept, width).transpose(1, 2, 3, 0, 4)
-    modes = unscaled / divisor[:, None, :, None, None]
-    return (modes, energies)
+    modes, energies = reduce_modes(
+        snapshots.transpose(0, 2, 1, 3), weights, eigenvectors.transpose(0, 1, 3, 2),
+        frequencies, offsets,
+    )
+    return (modes.transpose(0, 1, 3, 2, 4), energies)
 
 
 def fits(mesh):

time: 54 us -> 49.1 us (0.909)
  other arithmetic: 4.89 us -> 0 us
  between operations: 2.05 us -> 0.64 us
  Pallas kernels: 44.2 us -> 45.4 us
    unnamed x2, local copies, waits for them, and re-layouts: 0.01 us -> 2.84 us
    reshape x3 -> x0, local copies, waits for them, and re-layouts: 1.89 us -> none  [the longest x1 0.96 us: local_kernel(): raw.reshape(num_vars, owned, 2, modes_kept, width).transpose(1, 2, 3, 0, 4)]
    reduce_sum x3 -> x0, other arithmetic: 1.51 us -> none  [the longest x1 0.84 us: local_kernel(): lane_sum = jnp.sum(sums, axis=1)]
    pallas_call x1, Pallas kernels: 44.2 us -> 45.4 us  [reduce_modes(): pl.pallas_call(functools.partial(reduce_kernel, depth, num_blocks), out_s...]
    mul x1 -> x0, other arithmetic: 1 us -> none  [projection(): cosine = own_window * jnp.cos(angles)]
    div x1 -> x0, other arithmetic: 0.76 us -> none  [local_kernel(): modes = unscaled / divisor[:, None, :, None, None]]
    select_n x1 -> x0, other arithmetic: 0.74 us -> none  [projection(): shifted = (own[None, :] + offsets[:, None]) % count]
    sqrt x1 -> x0, other arithmetic: 0.59 us -> none  [local_kernel(): divisor = jnp.sqrt(num_blocks * energies + 1e-06)]
where the time goes in v2:
time: 49.1 us; the launch traced here: 48.9 us
  Pallas kernels  45.4 us (92%)
  local copies, waits for them, and re-layouts  2.84 us (6%)
  between operations  0.64 us (1%)
    pallas_call x1, Pallas kernels, reduce_modes(): pl.pallas_call(functools.partial(reduce_kernel, depth, num_blocks), out_s...  45.4 us
    unnamed x2, local copies, waits for them, and re-layouts  2.84 us

profile of v2, /device:TPU:0, one launch (start us, length us, event | category | flops | bytes accessed | tf_op | source)
XLA Modules:
  0.0 48.9 jit_solution(16903315062415951529)
XLA Ops:
  0.6 45.4 %shard_map.68 = (f32[4,2,5,4,256]{4,3,2,1,0:T(4,128)}, f32[4,4]{1,0:T(4,128)}) custom-call(f32[8,5,32,2048]{3,2,1,0:T(8,128)} %bitcast.3, f32[5,256]{1,0:T(8,128)} %w_hbm.1, f32[16,2,4,32]{3,2,1,0:T(4,128)} %bitcast.5, s32[16]{0:T(128)} %freq_hbm.1, s32[8]{0:T(128)} %off_hbm.1), custom_call_target="tpu_custom_call" | custom-call | tf_op jit(solution)/shard_map/pallas_call | solution.py:302
  46.1 1.6 %copy.9 = f32[4,2,4,5,256]{4,2,3,1,0:T(4,128)} copy(f32[4,2,4,5,256]{4,2,3,1,0:T(4,128)} %bitcast.4) | data formatting | bytes 327680
  47.7 1.2 %copy.10 = f32[4,4]{1,0:T(4,128)} copy(f32[4,4]{1,0:T(4,128)} %get-tuple-element.9) | data formatting | bytes 128

commit v3 on v2

--- a/solution.py
+++ b/solution.py
@@ -112,9 +112,11 @@
         copy = pltpu.make_async_copy(src, dst, in_sem.at[k])
         copy.start()
         small.append(copy)
+    chunks = [(d, v) for d in list(range(1, depth)) + [0] for v in range(num_vars)]
     loads = []
-    for v in range(num_vars):
-        load = pltpu.make_async_copy(x_ref.at[:, v], xbuf.at[v], x_sem.at[v])
+    for q, (d, v) in enumerate(chunks):
+        cols = pl.ds(pl.multiple_of(lax.rem(z + d, depth) * (2 * width), 2 * width), 2 * width)
+        load = pltpu.make_async_copy(x_ref.at[:, v, :, cols], xbuf.at[q], x_sem.at[q])
         load.start()
         loads.append(load)
 
@@ -139,25 +141,24 @@
             acat[0, (ca + c) % 2, (ya + y) % 2] = high[first : first + rows]
             acat[1, (ca + c) % 2, (ya + y) % 2] = low[first : first + rows]
 
-    def project(v):
-        def column(k, carry):
-            for xa in range(2):
-                xr = (x + xa) % 2
-                cols = pl.ds(pl.multiple_of(k * (2 * width) + xa * width, width), width)
-                block = xbuf[v, :, :, cols].reshape(inner, width)
-                high = block.astype(jnp.bfloat16)
-                low = (block - high.astype(jnp.float32)).astype(jnp.bfloat16)
-                both = jnp.dot(acat[...].reshape(2 * total_rows, inner), high, preferred_element_type=jnp.float32)
-                rest = jnp.dot(acat[0].reshape(total_rows, inner), low, preferred_element_type=jnp.float32)
-                res = both[:total_rows] + (both[total_rows:] + rest)
-                for cr, buf in ((0, keep), (1, send0)):
-                    for yr in range(2):
-                        first = (cr * 2 + yr) * rows
-                        buf[v, 0, xr, yr, k] = res[first : first + half]
-                        buf[v, 1, yr, xr, k] = res[first + half : first + rows]
-            return carry
-
-        lax.fori_loop(0, depth, column, 0)
+    def project(q):
+        for xa in range(2):
+            xr = (x + xa) % 2
+            block = xbuf[q, :, :, xa * width : (xa + 1) * width].reshape(inner, width)
+            high = block.astype(jnp.bfloat16)
+            low = (block - high.astype(jnp.float32)).astype(jnp.bfloat16)
+            both = jnp.dot(
+                acat[...].reshape(2 * total_rows, inner), high, preferred_element_type=jnp.float32
+            )
+            rest = jnp.dot(
+                acat[0].reshape(total_rows, inner), low, preferred_element_type=jnp.float32
+            )
+            res = both[:total_rows] + (both[total_rows:] + rest)
+            for cr, buf in ((0, keep), (1, send0)):
+                for yr in range(2):
+                    first = (cr * 2 + yr) * rows
+                    buf[q, 0, xr, yr] = res[first : first + half]
+                    buf[q, 1, yr, xr] = res[first + half : first + rows]
 
     def remote(src, dst, sem_out, sem_in, target):
         return pltpu.make_async_remote_copy(
@@ -165,68 +166,63 @@
             device_id=target, device_id_type=MESH,
         )
 
+    count = len(chunks)
     hop0 = [
-        remote(send0.at[v], r0.at[v], s0_sem.at[v], t0_sem.at[v], across_core)
-        for v in range(num_vars)
+        remote(send0.at[q], r0.at[q], s0_sem.at[q], t0_sem.at[q], across_core)
+        for q in range(count)
     ]
     hop1 = [
         [
-            remote(keep.at[v, h, 1], r1.at[v, h], s1_sem.at[v, h], t1_sem.at[v, h], to)
+            remote(keep.at[q, h, 1], r1.at[q, h], s1_sem.at[q, h], t1_sem.at[q, h], to)
             for h, to in ((0, across_x), (1, across_y))
         ]
-        for v in range(num_vars)
+        for q in range(count)
     ]
     hop2 = [
         [
-            remote(r1.at[v, h, 1], r2.at[v, h], s2_sem.at[v, h], t2_sem.at[v, h], to)
+            remote(r1.at[q, h, 1], r2.at[q, h], s2_sem.at[q, h], t2_sem.at[q, h], to)
             for h, to in ((0, across_y), (1, across_x))
         ]
-        for v in range(num_vars)
+        for q in range(count)
     ]
-    hop3 = []
-    for v in range(num_vars):
-        group = []
+    hop3 = {}
+    for q, (d, v) in enumerate(chunks):
+        if d:
+            hop3[d, v] = remote(
+                s2.at[q], r3.at[v, d - 1], s3_sem.at[v, d - 1], t3_sem.at[v, d - 1],
+                (lax.rem(z + d, depth) * 2 + x, blk),
+            )
+
+    def stage0(q):
+        loads[q].wait()
+        project(q)
+        if q == 0:
+            pl.semaphore_wait(barrier, size + 1)
+        hop0[q].start()
+
+    def stage1(q):
+        hop0[q].wait_recv()
+        for h in range(2):
+            keep[q, h, 1] = keep[q, h, 1] + r0[q, h, 1]
+            hop1[q][h].start()
+
+    def stage2(q):
+        for h in range(2):
+            hop1[q][h].wait_recv()
+            r1[q, h, 1] = r1[q, h, 1] + (keep[q, h, 0, 1] + r0[q, h, 0, 1])
+            hop2[q][h].start()
+
+    def stage3(q):
+        for h in range(2):
+            hop2[q][h].wait_recv()
+            s2[q, h] = (keep[q, h, 0, 0] + r0[q, h, 0, 0]) + (r1[q, h, 0] + r2[q, h])
+        d, v = chunks[q]
+        if d:
+            hop3[d, v].start()
+            return
+        result = s2[q]
         for d in range(1, depth):
-            k = lax.rem(z + d, depth)
-            group.append(
-                remote(
-                    s2.at[v, k], r3.at[v, d - 1], s3_sem.at[v, d - 1], t3_sem.at[v, d - 1],
-                    (k * 2 + x, blk),
-                )
-            )
-        hop3.append(group)
-
-    def stage0(v):
-        loads[v].wait()
-        project(v)
-        if v == 0:
-            pl.semaphore_wait(barrier, size + 1)
-        hop0[v].start()
-
-    def stage1(v):
-        hop0[v].wait_recv()
-        for h in range(2):
-            keep[v, h, 1] = keep[v, h, 1] + r0[v, h, 1]
-            hop1[v][h].start()
-
-    def stage2(v):
-        for h in range(2):
-            hop1[v][h].wait_recv()
-            r1[v, h, 1] = r1[v, h, 1] + (keep[v, h, 0, 1] + r0[v, h, 0, 1])
-            hop2[v][h].start()
-
-    def stage3(v):
-        for h in range(2):
-            hop2[v][h].wait_recv()
-            s2[v, :, h] = (keep[v, h, 0, 0] + r0[v, h, 0, 0]) + (r1[v, h, 0] + r2[v, h])
-        for copy in hop3[v]:
-            copy.start()
-
-    def stage4(v):
-        for copy in hop3[v]:
-            copy.wait_recv()
-        result = s2[v, z]
-        for d in range(1, depth):
+            hop3[d, v].wait_recv()
             result = result + r3[v, d - 1]
         result = result.reshape(rows, width)
         raw[v] = result
@@ -236,10 +232,10 @@
         else:
             acc[...] = acc[...] + term
 
-    stages = (stage0, stage1, stage2, stage3, stage4)
-    for step in range(num_vars + len(stages) - 1):
-        for lag, stage in enumerate(stages):
-            if 0 <= step - lag < num_vars:
+    lags = (0, 2, 5, 8)
+    for step in range(count + lags[-1]):
+        for lag, stage in zip(lags, (stage0, stage1, stage2, stage3)):
+            if 0 <= step - lag < count:
                 stage(step - lag)
 
     def fold(value):
@@ -248,9 +244,15 @@
             folded = folded + value[:, k * LANES : (k + 1) * LANES]
         return folded
 
-    esend[:rows, :] = fold(acc[...])
+    diagonal = lax.broadcasted_iota(jnp.int32, (rows, LANES), 0) == lax.broadcasted_iota(
+        jnp.int32, (rows, LANES), 1
+    )
+    last = lax.broadcasted_iota(jnp.int32, (1, LANES), 1) == rows
+    row_sum = jnp.sum(fold(acc[...]), axis=1, keepdims=True)
     weight_sum = fold(jnp.sum(w_ref[...], axis=0, keepdims=True))
-    esend[rows:, :] = jnp.broadcast_to(weight_sum, (8, LANES))
+    weight_sum = jnp.sum(weight_sum, axis=1, keepdims=True)
+    lane_sum = jnp.sum(jnp.where(diagonal, row_sum, 0.0), axis=0, keepdims=True)
+    esend[...] = jnp.where(last, weight_sum, lane_sum)
     share = []
     for d in range(1, size):
         copy = remote(
@@ -264,10 +266,11 @@
         share[d - 1].wait_recv()
         total = total + erecv[d - 1]
     owned = rows // (2 * modes_kept)
-    pair = total[:rows].reshape(owned, 2 * modes_kept, LANES)
+    weight_total = jnp.sum(jnp.where(last, total, 0.0), axis=1, keepdims=True)
+    pair = jnp.sum(jnp.where(diagonal, total, 0.0), axis=1, keepdims=True)
+    pair = pair.reshape(owned, 2 * modes_kept, 1)
     pair = pair + jnp.concatenate([pair[:, modes_kept:], pair[:, :modes_kept]], axis=1)
-    weight_total = jnp.sum(total[rows : rows + 1], axis=1, keepdims=True)
-    energy = jnp.sum(pair, axis=2, keepdims=True) / (num_blocks * weight_total)[None]
+    energy = pair / (num_blocks * weight_total)[None]
     inverse = 1.0 / jnp.sqrt(num_blocks * energy + 1e-06)
     for v in range(num_vars):
         scaled = raw[v].reshape(owned, 2 * modes_kept, width) * inverse
@@ -277,11 +280,11 @@
     same = lax.broadcasted_iota(jnp.int32, square, 0) == lax.broadcasted_iota(jnp.int32, square, 1)
     spread = jnp.broadcast_to(energy[:, :modes_kept], (owned, modes_kept, modes_kept))
     energy_ref[...] = jnp.sum(jnp.where(same[None], spread, 0.0), axis=1)
-    for v in range(num_vars):
-        hop0[v].wait_send()
-        for copy in hop1[v] + hop2[v] + hop3[v]:
+    for q in range(count):
+        hop0[q].wait_send()
+        for copy in hop1[q] + hop2[q]:
             copy.wait_send()
-    for copy in share:
+    for copy in list(hop3.values()) + share:
         copy.wait_send()
 
 
@@ -295,6 +298,7 @@
     inner = items * times
     half = rows // 2
     size = 2 * depth
+    chunks = depth * num_vars
     f32 = jnp.float32
     dma = pltpu.SemaphoreType.DMA
     anywhere = pl.BlockSpec(memory_space=pl.ANY)
@@ -308,31 +312,31 @@
         in_specs=[anywhere] * 5,
         out_specs=(vmem, vmem),
         scratch_shapes=[
-            pltpu.VMEM((num_vars, items, times, cells), f32),
+            pltpu.VMEM((chunks, items, times, 2 * width), f32),
             pltpu.VMEM((num_vars, width), f32),
             pltpu.VMEM(vectors.shape, f32),
             pltpu.SMEM(frequencies.shape, jnp.int32),
             pltpu.SMEM(offsets.shape, jnp.int32),
             pltpu.VMEM((num_vars, rows, width), f32),
             pltpu.VMEM((2, 2, 2, rows, inner), jnp.bfloat16),
-            pltpu.VMEM((num_vars, 2, 2, 2, depth, half, width), f32),
-            pltpu.VMEM((num_vars, 2, 2, 2, depth, half, width), f32),
-            pltpu.VMEM((num_vars, 2, 2, 2, depth, half, width), f32),
-            pltpu.VMEM((num_vars, 2, 2, depth, half, width), f32),
-            pltpu.VMEM((num_vars, 2, depth, half, width), f32),
-            pltpu.VMEM((num_vars, depth, 2, half, width), f32),
+            pltpu.VMEM((chunks, 2, 2, 2, half, width), f32),
+            pltpu.VMEM((chunks, 2, 2, 2, half, width), f32),
+            pltpu.VMEM((chunks, 2, 2, 2, half, width), f32),
+            pltpu.VMEM((chunks, 2, 2, half, width), f32),
+            pltpu.VMEM((chunks, 2, half, width), f32),
+            pltpu.VMEM((chunks, 2, half, width), f32),
             pltpu.VMEM((num_vars, depth - 1, 2, half, width), f32),
             pltpu.VMEM((rows, width), f32),
-            pltpu.VMEM((rows + 8, LANES), f32),
-            pltpu.VMEM((size - 1, rows + 8, LANES), f32),
+            pltpu.VMEM((1, LANES), f32),
+            pltpu.VMEM((size - 1, 1, LANES), f32),
             dma((4,)),
-            dma((num_vars,)),
-            dma((num_vars,)),
-            dma((num_vars,)),
-            dma((num_vars, 2)),
-            dma((num_vars, 2)),
-            dma((num_vars, 2)),
-            dma((num_vars, 2)),
+            dma((chunks,)),
+            dma((chunks,)),
+            dma((chunks,)),
+            dma((chunks, 2)),
+            dma((chunks, 2)),
+            dma((chunks, 2)),
+            dma((chunks, 2)),
             dma((num_vars, depth - 1)),
             dma((num_vars, depth - 1)),
             dma((size - 1,)),

time: 49.1 us -> 42.9 us (0.87)
  Pallas kernels: 45.4 us -> 39.3 us
    pallas_call x1, Pallas kernels: 45.4 us -> 39.3 us  [reduce_modes(): pl.pallas_call(functools.partial(reduce_kernel, depth, num_blocks), out_s...]
where the time goes in v3:
time: 42.9 us; the launch traced here: 42.7 us
  Pallas kernels  39.3 us (92%)
  local copies, waits for them, and re-layouts  2.84 us (7%)
  between operations  0.64 us (1%)
    pallas_call x1, Pallas kernels, reduce_modes(): pl.pallas_call(functools.partial(reduce_kernel, depth, num_blocks), out_s...  39.3 us
    unnamed x2, local copies, waits for them, and re-layouts  2.84 us

profile of v3, /device:TPU:0, one launch (start us, length us, event | category | flops | bytes accessed | tf_op | source)
XLA Modules:
  0.0 42.7 jit_solution(13988791437600276150)
XLA Ops:
  0.6 39.3 %shard_map.68 = (f32[4,2,5,4,256]{4,3,2,1,0:T(4,128)}, f32[4,4]{1,0:T(4,128)}) custom-call(f32[8,5,32,2048]{3,2,1,0:T(8,128)} %bitcast.3, f32[5,256]{1,0:T(8,128)} %w_hbm.1, f32[16,2,4,32]{3,2,1,0:T(4,128)} %bitcast.5, s32[16]{0:T(128)} %freq_hbm.1, s32[8]{0:T(128)} %off_hbm.1), custom_call_target="tpu_custom_call" | custom-call | tf_op jit(solution)/shard_map/pallas_call | solution.py:306
  39.9 1.6 %copy.9 = f32[4,2,4,5,256]{4,2,3,1,0:T(4,128)} copy(f32[4,2,4,5,256]{4,2,3,1,0:T(4,128)} %bitcast.4) | data formatting | bytes 327680
  41.5 1.2 %copy.10 = f32[4,4]{1,0:T(4,128)} copy(f32[4,4]{1,0:T(4,128)} %get-tuple-element.9) | data formatting | bytes 128
